TPU v7x, 128 devices: a whole 4x4x4 slice. The times are simulated.
128 devices in a mesh: blk: 8 (over x, core), narrow: 16 (over y, z).
Axes of the slice: x: 4, y: 4, z: 4, core: 2. Of those that a mesh axis runs over, the one named last changes fastest.
Arguments:
- node_feats: bfloat16 [262144, 128], P(('blk', 'narrow')), may hold values from -6 to 6
- history: bfloat16 [262144, 1024], P(('blk', 'narrow')), may hold values from -6 to 6
- tile_src: int32 [2048, 2], P(('blk', 'narrow')), may hold values from 0 to 2047, as said below
- tile_count: int32 [2048], P(('blk', 'narrow')), may hold values from 1 to 2
- tile_edges: bfloat16 [2048, 2, 128, 128], P(('blk', 'narrow')), may hold values from 0 to 1, as said below
- w1_self: bfloat16 [128, 1024], replicated, may hold values from -0.5 to 0.5
- w1_nbr: bfloat16 [128, 1024], replicated, may hold values from -0.5 to 0.5
- bias_one: float32 [1024], replicated, may hold values from -3 to 3
- gain_one: float32 [1024], replicated, may hold values from 0.5 to 1.5
- w2_self: bfloat16 [1024, 1024], replicated, may hold values from -0.1875 to 0.1875
- w2_nbr: bfloat16 [1024, 1024], replicated, may hold values from -0.1875 to 0.1875
- bias_two: float32 [1024], replicated, may hold values from -3 to 3
- gain_two: float32 [1024], replicated, may hold values from 0.5 to 1.5
Outputs:
- fresh_history: bfloat16 [262144, 1024], P(('blk', 'narrow'))
- embeddings: bfloat16 [262144, 1024], P(('blk', 'narrow'))
Inputs may be any that keep to these rules, and one draw needn't show every extreme that they name: `tile_src`: node block g is stored on device g // 16 of the order blk+narrow (blk slowest), as its block g % 16. For the 16 block rows of one device (r, m), exactly 1 of its tiles name blocks of each device (r, m2) and exactly 1 name blocks of each device ((r + 1) % 8, m2), for all 16 values of m2. `tile_edges`: every entry is 0 or 1; tiles past tile_count are padding and hold arbitrary entries.
All inputs are finite; a program needn't handle non-finite values.
Results may differ from a plain program's by a relative error of at most 0.0045.
Values may be sent and summed in bfloat16 or wider, within the bound.
A program may use at most 128 MiB of HBM per device.

v0:
```python
import jax
import jax.numpy as jnp
from jax import lax
from jax.sharding import PartitionSpec as P


def shifted(block, axis, distance):
    devices = range(lax.axis_size(axis))
    route = [((i - distance) % len(devices), i) for i in devices]
    return lax.ppermute(block, axis, route)


def rms_relu(values, gain_row):
    inv_scale = lax.rsqrt(jnp.mean(values * values, axis=-1, keepdims=True) + 1e-06)
    return jax.nn.relu(values * inv_scale * gain_row).astype(jnp.bfloat16)


def sage_layer(self_rows, mean_rows, w_self, w_neighbour, bias_row, gain_row):
    summed = jnp.dot(self_rows, w_self, preferred_element_type=jnp.float32)
    summed = summed + jnp.dot(mean_rows, w_neighbour, preferred_element_type=jnp.float32)
    return rms_relu(summed + bias_row, gain_row)


def neighbour_means(tile_rows, live_edges, degree):
    summed = jnp.einsum("ltij,ltjw->liw", live_edges, tile_rows, preferred_element_type=jnp.float32)
    averaged = (summed / degree[:, :, None]).astype(jnp.bfloat16)
    return averaged.reshape(-1, tile_rows.shape[-1])


def place_slots(route_key, per_slot, source_local, tile_total, slot_total):
    positions = jnp.arange(tile_total, dtype=jnp.int32)
    earlier = (route_key[:, None] == route_key[None, :]) & (positions[:, None] > positions[None, :])
    slot_index = route_key * per_slot + jnp.sum(earlier.astype(jnp.int32), axis=1)
    slot_ids = jnp.arange(slot_total, dtype=jnp.int32)
    placed = (slot_index[:, None] == slot_ids[None, :]).astype(jnp.int32)
    requests = jnp.sum(placed * source_local[:, None], axis=0)
    return (slot_index, requests)


def body(
    node_feats,
    history,
    tile_src,
    tile_count,
    tile_edges,
    w1_self,
    w1_nbr,
    bias_one,
    gain_one,
    w2_self,
    w2_nbr,
    bias_two,
    gain_two,
):
    block_count, tile_width = tile_src.shape
    block_rows = tile_edges.shape[2]
    cycle_size = lax.axis_size("blk")
    peer_count = lax.axis_size("narrow")
    tile_total = block_count * tile_width
    per_peer = tile_total // (2 * peer_count)
    flat_src = tile_src.reshape(tile_total)
    source_device = flat_src // block_count
    source_local = flat_src % block_count
    feat_blocks = node_feats.reshape(block_count, block_rows, node_feats.shape[1])
    hist_blocks = history.reshape(block_count, block_rows, history.shape[1])
    row_step = (source_device // peer_count - lax.axis_index("blk")) % cycle_size
    route_key = source_device % peer_count * 2 + row_step
    slot_index, requests = place_slots(route_key, per_peer, source_local, tile_total, tile_total)
    requests = requests.reshape(peer_count, 2 * per_peer)
    near_req = requests[:, :per_peer]
    far_req = shifted(requests[:, per_peer:], "blk", 1)
    asked_ids = lax.all_to_all(
        jnp.concatenate([near_req, far_req], axis=1),
        "narrow",
        split_axis=0,
        concat_axis=0,
        tiled=True,
    )
    served_feats, served_hist = (
        lax.all_to_all(feat_blocks[asked_ids], "narrow", split_axis=0, concat_axis=0, tiled=True),
        lax.all_to_all(hist_blocks[asked_ids], "narrow", split_axis=0, concat_axis=0, tiled=True),
    )
    back_feats, back_hist = shifted(
        (served_feats[:, per_peer:], served_hist[:, per_peer:]), "blk", -1
    )
    got_feats = jnp.concatenate([served_feats[:, :per_peer], back_feats], axis=1)
    got_hist = jnp.concatenate([served_hist[:, :per_peer], back_hist], axis=1)
    tile_feats = got_feats.reshape(tile_total, block_rows, node_feats.shape[1])[slot_index]
    tile_feats = tile_feats.reshape(block_count, tile_width, block_rows, node_feats.shape[1])
    tile_hist = got_hist.reshape(tile_total, block_rows, history.shape[1])[slot_index]
    tile_hist = tile_hist.reshape(block_count, tile_width, block_rows, history.shape[1])
    live_tiles = (jnp.arange(tile_width, dtype=jnp.int32)[None, :] < tile_count[:, None]).astype(
        tile_edges.dtype
    )
    live_edges = tile_edges * live_tiles[:, :, None, None]
    degree = jnp.maximum(jnp.sum(live_edges, axis=(1, 3), dtype=jnp.float32), 1.0)
    mean_feats = neighbour_means(tile_feats, live_edges, degree)
    mean_hist = neighbour_means(tile_hist, live_edges, degree)
    fresh_rows = sage_layer(node_feats, mean_feats, w1_self, w1_nbr, bias_one, gain_one)
    embed_rows = sage_layer(fresh_rows, mean_hist, w2_self, w2_nbr, bias_two, gain_two)
    return (fresh_rows, embed_rows)


def solution(mesh):
    return jax.shard_map(
        body,
        mesh=mesh,
        in_specs=(
            P(("blk", "narrow"), None),
            P(("blk", "narrow"), None),
            P(("blk", "narrow"), None),
            P(("blk", "narrow")),
            P(("blk", "narrow"), None, None, None),
            P(),
            P(),
            P(),
            P(),
            P(),
            P(),
            P(),
            P(),
        ),
        out_specs=(P(("blk", "narrow"), None), P(("blk", "narrow"), None)),
        check_vma=False,
    )
```

profile of v0, /device:TPU:1, one launch (start us, length us, event | category | flops | bytes accessed | tf_op | source)
XLA Modules:
  0.0 298.7 jit_solution(5677695067480341973)
XLA Ops:
  0.6 0.0 copy-start
  0.6 0.9 copy.36
  1.6 0.1 reshape.413
  1.7 0.2 convert_reduce_fusion.1
  1.9 0.1 select_reduce_fusion
  2.0 0.1 reshape.414
  2.0 0.1 fusion.17
  2.1 2.6 collective-permute-start
  4.7 0.1 copy.37
  4.8 0.7 collective-permute-done
  5.5 0.1 copy.38
  5.6 0.1 copy.39
  5.7 14.0 %all_to_all.22 = s32[16,1,2]{2,1,0:T(1,128)S(1)} all-to-all(s32[16,1,2]{2,1,0:T(1,128)S(1)} %copy.39), channel_id=1, replica_groups=mesh['blk'=8,'narrow'=16] {'narrow'}, dimensions={0} | all-to-all | bytes 256 | tf_op jit(solution)/shard_map/all_to_all | solution.py:72
  19.7 0.1 copy.40
  19.8 0.1 copy.41
  19.9 0.1 reshape.425
  20.0 7.1 %gather_fusion.2 = bf16[32,128,1024]{2,1,0:T(8,128)(2,1)} fusion(bf16[16,128,1024]{2,1,0:T(8,128)(2,1)} %bitcast.44, s32[1024]{0:T(1024)S(1)} %pad_clamp_fusion.1), kind=kCustom, calls=%fused_computation.2 | custom fusion | bytes 16777344 | tf_op jit(solution)/shard_map/gather | solution.py:81
  27.0 0.0 copy-start.10
  27.0 4.9 %all-to-all-start.2 = ((bf16[16,2,128,1024]{3,2,1,0:T(8,128)(2,1)}), bf16[16,2,128,1024]{3,2,1,0:T(8,128)(2,1)}, u32[]{:S(2)}, u32[]{:S(2)}) async-start(bf16[16,2,128,1024]{3,2,1,0:T(8,128)(2,1)} %bitcast.43), calls=%async_computation.2 | async-start | bytes 16777216 | tf_op jit(solution)/shard_map/all_to_all | solution.py:81
  31.9 0.1 reshape.416
  32.0 0.0 copy-done.10
  32.0 0.1 fusion.6
  32.1 0.0 copy-done.2
  32.1 1.7 gather_fusion
  33.7 114.3 %all-to-all-done.2 = bf16[16,2,128,1024]{3,2,1,0:T(8,128)(2,1)} async-done(((bf16[16,2,128,1024]{3,2,1,0:T(8,128)(2,1)}), bf16[16,2,128,1024]{3,2,1,0:T(8,128)(2,1)}, u32[]{:S(2)}, u32[]{:S(2)}) %all-to-all-start.2) | async-done | bytes 8388640 | tf_op jit(solution)/shard_map/all_to_all | solution.py:81
  148.0 8.6 %all-to-all-start.1 = ((bf16[16,2,128,128]{3,2,1,0:T(8,128)(2,1)}), bf16[16,2,128,128]{3,2,1,0:T(8,128)(2,1)}, u32[]{:S(2)}, u32[]{:S(2)}) async-start(bf16[16,2,128,128]{3,2,1,0:T(8,128)(2,1)} %bitcast.48), calls=%async_computation.1 | async-start | bytes 2097152 | tf_op jit(solution)/shard_map/all_to_all | solution.py:80
  156.7 0.0 copy-start.3
  156.7 0.0 copy-start.6
  156.7 6.1 %fusion.15 = (bf16[16,1,128,1024]{3,2,1,0:T(8,128)(2,1)}, bf16[16,1,128,1024]{3,2,1,0:T(8,128)(2,1)}) fusion(bf16[16,2,128,1024]{3,2,1,0:T(8,128)(2,1)} %all-to-all-done.2), kind=kLoop, calls=%fused_computation.69 | loop fusion | bytes 16777216 | tf_op jit(solution)/shard_map/slice | solution.py:87
  162.9 6.0 %collective-permute-start.2 = (bf16[16,1,128,1024]{3,2,1,0:T(8,128)(2,1)}, bf16[16,1,128,1024]{3,2,1,0:T(8,128)(2,1)}, u32[]{:S(2)}, u32[]{:S(2)}) collective-permute-start(bf16[16,1,128,1024]{3,2,1,0:T(8,128)(2,1)} %get-tuple-element.11), channel_id=1, source_target_pairs={{16,0},{32,16},{48,32},{64,48},{80,64},{96,80},{112,96},{0,112},{1... | collective-permute-start | bytes 12582920 | tf_op jit(solution)/shard_map/ppermute | solution.py:10
  168.8 0.0 copy-done.3
  168.8 0.6 convert_reduce_fusion
  169.4 0.0 all-to-all-done.1
  169.4 1.3 fusion.16
  170.7 6.1 %collective-permute-start.1 = (bf16[16,1,128,128]{3,2,1,0:T(8,128)(2,1)S(1)}, bf16[16,1,128,128]{3,2,1,0:T(8,128)(2,1)S(1)}, u32[]{:S(2)}, u32[]{:S(2)}) collective-permute-start(bf16[16,1,128,128]{3,2,1,0:T(8,128)(2,1)S(1)} %get-tuple-element.13), channel_id=1, source_target_pairs={{16,0},{32,16},{48,32},{64,48},{80,64},{96,80},{112,96},{0,112},{1... | collective-permute-start | bytes 1572872 | tf_op jit(solution)/shard_map/ppermute | solution.py:10
  176.9 0.0 copy-done.6
  176.9 0.0 copy-start.5
  176.9 0.0 copy-start.9
  176.9 4.5 %fusion.18 = f32[2048,1024]{0,1:T(8,128)} fusion(bf16[2048,128]{1,0:T(8,128)(2,1)S(1)} %copy-done.2, bf16[128,1024]{1,0:T(8,128)(2,1)S(1)} %copy-done.6), kind=kOutput, calls=%fused_computation.72 | convolution fusion | flops 536870912 | bytes 9175040 | tf_op jit(solution)/shard_map/dot_general | solution.py:19
  181.4 52.0 %collective-permute-done.1 = bf16[16,1,128,128]{3,2,1,0:T(8,128)(2,1)S(1)} collective-permute-done((bf16[16,1,128,128]{3,2,1,0:T(8,128)(2,1)S(1)}, bf16[16,1,128,128]{3,2,1,0:T(8,128)(2,1)S(1)}, u32[]{:S(2)}, u32[]{:S(2)}) %collective-permute-start.1) | collective-permute-done | bytes 524320 | tf_op jit(solution)/shard_map/ppermute | solution.py:10
  233.4 0.1 pad_maximum_fusion.1
  233.5 1.7 gather_fusion.1
  235.2 2.0 divide_convert_fusion
  237.2 0.0 copy-done.5
  237.2 0.0 copy-done.9
  237.2 0.0 copy-start.7
  237.2 4.4 %multiply_reduce_fusion.1 = (f32[2048]{0:T(1024)S(1)}, f32[2048,1024]{0,1:T(8,128)S(1)}) fusion(f32[1024]{0:T(1024)S(1)} %copy-done.9, f32[2048,1024]{0,1:T(8,128)} %fusion.18, bf16[2048,128]{1,0:T(8,128)(2,1)S(1)} %bitcast.50, bf16[128,1024]{1,0:T(8,128)(2,1)S(1)} %copy-done.5), kind=kOutput, calls=%fused_computation.11 | convolution fusion | flops 545257472 | bytes 17575936 | tf_op jit(solution)/shard_map/dot_general | solution.py:20
  241.6 0.0 copy-done.7
  241.6 3.0 %maximum_convert_fusion.1 = bf16[2048,1024]{0,1:T(8,128)(2,1)} fusion(f32[2048,1024]{0,1:T(8,128)S(1)} %get-tuple-element.19, f32[1024]{0:T(1024)S(1)} %copy-done.7, f32[2048]{0:T(1024)S(1)} %add_rsqrt_fusion.1), kind=kLoop, calls=%fused_computation.10 | loop fusion | flops 8388608 | bytes 12595200 | tf_op jit(solution)/shard_map/convert_element_type | solution.py:15
  244.6 6.4 %copy.43 = bf16[2048,1024]{1,0:T(8,128)(2,1)} copy(bf16[2048,1024]{0,1:T(8,128)(2,1)} %maximum_convert_fusion.1) | data formatting | bytes 8388608
  251.0 10.8 %fusion.19 = f32[2048,1024]{0,1:T(8,128)} fusion(bf16[2048,1024]{0,1:T(8,128)(2,1)} %maximum_convert_fusion.1, bf16[1024,1024]{1,0:T(8,128)(2,1)} %param.22), kind=kOutput, calls=%fused_computation.73 | convolution fusion | flops 4294967296 | bytes 14680064 | tf_op jit(solution)/shard_map/dot_general | solution.py:19
  261.8 0.0 collective-permute-done.2
  261.8 0.0 copy-done.1
  261.8 6.2 %pad_maximum_fusion = bf16[16,2,128,1024]{3,2,1,0:T(8,128)(2,1)} fusion(bf16[16,1,128,1024]{3,2,1,0:T(8,128)(2,1)} %collective-permute-done.2, bf16[16,1,128,1024]{3,2,1,0:T(8,128)(2,1)S(1)} %copy-done.1), kind=kLoop, calls=%fused_computation.4 | loop fusion | flops 4194304 | bytes 16777216 | tf_op jit(solution)/shard_map/concatenate | solution.py:87
  268.0 8.5 %gather_fusion.3 = bf16[32,128,1024]{2,1,0:T(8,128)(2,1)} fusion(bf16[32,128,1024]{2,1,0:T(8,128)(2,1)} %bitcast.42, s32[1024]{0:T(1024)S(1)} %pad_clamp_fusion), kind=kCustom, calls=%fused_computation.3 | custom fusion | bytes 16777344 | tf_op jit(solution)/shard_map/gather | solution.py:90
  276.5 0.0 copy-done.4
  276.5 4.7 %fusion = bf16[16,128,1024]{2,1,0:T(8,128)(2,1)S(1)} fusion(f32[16,128]{1,0:T(8,128)S(1)} %broadcast_maximum_fusion, bf16[16,2,128,1024]{3,2,1,0:T(8,128)(2,1)} %bitcast.45, bf16[16,2,128,128]{3,2,1,0:T(8,128)(2,1)S(1)} %copy-done.4, bf16[16,2]{1,0:T(8,128)(2,1)S(1)} %fusion.6), kind=kOutput, calls=%fused_computation.6 | convolution fusion | flops 1078460416 | bytes 13639744 | tf_op jit(solution)/shard_map/ltij,ltjw->liw/dot_general | solution.py:25
  281.2 0.0 copy-done
  281.2 0.0 copy-done.11
  281.3 0.0 copy-start.8
  281.3 8.1 %multiply_reduce_fusion = (f32[2048]{0:T(1024)S(1)}, f32[2048,1024]{0,1:T(8,128)S(1)}) fusion(f32[1024]{0:T(1024)S(1)} %copy-done.11, f32[2048,1024]{0,1:T(8,128)} %fusion.19, bf16[2048,1024]{1,0:T(8,128)(2,1)S(1)} %bitcast.51, bf16[1024,1024]{1,0:T(8,128)(2,1)S(1)} %copy-done), kind=kOutput, calls=%fused_computation.8 | convolution fusion | flops 4303353856 | bytes 23080960 | tf_op jit(solution)/shard_map/dot_general | solution.py:20
  289.4 0.0 copy-done.8
  289.4 2.9 maximum_convert_fusion
  292.3 6.4 %copy.44 = bf16[2048,1024]{1,0:T(8,128)(2,1)} copy(bf16[2048,1024]{0,1:T(8,128)(2,1)} %maximum_convert_fusion) | data formatting | bytes 8388608
  (14 shorter events, 0.1 us)
Async XLA Ops:
  0.6 280.6 %copy-start = (bf16[1024,1024]{1,0:T(8,128)(2,1)S(1)}, bf16[1024,1024]{1,0:T(8,128)(2,1)}, u32[]{:S(2)}) copy-start(bf16[1024,1024]{1,0:T(8,128)(2,1)} %param.23) | copy-start | bytes 6291460
  2.1 3.4 %collective-permute-start = (s32[16,1]{1,0:T(8,128)S(1)}, s32[16,1]{1,0:T(8,128)S(1)}, u32[]{:S(2)}, u32[]{:S(2)}) collective-permute-start(s32[16,1]{1,0:T(8,128)S(1)} %get-tuple-element.15), channel_id=1, source_target_pairs={{112,0},{0,16},{16,32},{32,48},{48,64},{64,80},{80,96},{96,112},{1... | collective-permute-start | bytes 200 | tf_op jit(solution)/shard_map/ppermute | solution.py:10
  27.0 5.0 %copy-start.10 = (s32[16]{0:T(128)S(1)}, s32[16]{0:T(128)}, u32[]{:S(2)}) copy-start(s32[16]{0:T(128)} %param.16) | copy-start | bytes 196
  27.0 5.1 %copy-start.2 = (bf16[2048,128]{1,0:T(8,128)(2,1)S(1)}, bf16[2048,128]{1,0:T(8,128)(2,1)}, u32[]{:S(2)}) copy-start(bf16[2048,128]{1,0:T(8,128)(2,1)} %param.13) | copy-start | bytes 1572868
  27.0 121.0 %all-to-all-start.2 = ((bf16[16,2,128,1024]{3,2,1,0:T(8,128)(2,1)}), bf16[16,2,128,1024]{3,2,1,0:T(8,128)(2,1)}, u32[]{:S(2)}, u32[]{:S(2)}) async-start(bf16[16,2,128,1024]{3,2,1,0:T(8,128)(2,1)} %bitcast.43), calls=%async_computation.2 | async-start | bytes 16777216 | tf_op jit(solution)/shard_map/all_to_all | solution.py:81
  148.0 21.4 %all-to-all-start.1 = ((bf16[16,2,128,128]{3,2,1,0:T(8,128)(2,1)}), bf16[16,2,128,128]{3,2,1,0:T(8,128)(2,1)}, u32[]{:S(2)}, u32[]{:S(2)}) async-start(bf16[16,2,128,128]{3,2,1,0:T(8,128)(2,1)} %bitcast.48), calls=%async_computation.1 | async-start | bytes 2097152 | tf_op jit(solution)/shard_map/all_to_all | solution.py:80
  156.7 12.1 %copy-start.3 = (bf16[16,2,128,128]{3,2,1,0:T(8,128)(2,1)S(1)}, bf16[16,2,128,128]{3,2,1,0:T(8,128)(2,1)}, u32[]{:S(2)}) copy-start(bf16[16,2,128,128]{3,2,1,0:T(8,128)(2,1)} %param.17) | copy-start | bytes 3145732
  156.7 20.2 %copy-start.6 = (bf16[128,1024]{1,0:T(8,128)(2,1)S(1)}, bf16[128,1024]{1,0:T(8,128)(2,1)}, u32[]{:S(2)}) copy-start(bf16[128,1024]{1,0:T(8,128)(2,1)} %param.18) | copy-start | bytes 786436
  162.9 99.0 %collective-permute-start.2 = (bf16[16,1,128,1024]{3,2,1,0:T(8,128)(2,1)}, bf16[16,1,128,1024]{3,2,1,0:T(8,128)(2,1)}, u32[]{:S(2)}, u32[]{:S(2)}) collective-permute-start(bf16[16,1,128,1024]{3,2,1,0:T(8,128)(2,1)} %get-tuple-element.11), channel_id=1, source_target_pairs={{16,0},{32,16},{48,32},{64,48},{80,64},{96,80},{112,96},{0,112},{1... | collective-permute-start | bytes 12582920 | tf_op jit(solution)/shard_map/ppermute | solution.py:10
  170.7 62.7 %collective-permute-start.1 = (bf16[16,1,128,128]{3,2,1,0:T(8,128)(2,1)S(1)}, bf16[16,1,128,128]{3,2,1,0:T(8,128)(2,1)S(1)}, u32[]{:S(2)}, u32[]{:S(2)}) collective-permute-start(bf16[16,1,128,128]{3,2,1,0:T(8,128)(2,1)S(1)} %get-tuple-element.13), channel_id=1, source_target_pairs={{16,0},{32,16},{48,32},{64,48},{80,64},{96,80},{112,96},{0,112},{1... | collective-permute-start | bytes 1572872 | tf_op jit(solution)/shard_map/ppermute | solution.py:10
  176.9 60.3 %copy-start.5 = (bf16[128,1024]{1,0:T(8,128)(2,1)S(1)}, bf16[128,1024]{1,0:T(8,128)(2,1)}, u32[]{:S(2)}) copy-start(bf16[128,1024]{1,0:T(8,128)(2,1)} %param.19) | copy-start | bytes 786436
  176.9 60.3 %copy-start.9 = (f32[1024]{0:T(1024)S(1)}, f32[1024]{0:T(1024)}, u32[]{:S(2)}) copy-start(f32[1024]{0:T(1024)} %param.20) | copy-start | bytes 12292
  237.2 4.4 %copy-start.7 = (f32[1024]{0:T(1024)S(1)}, f32[1024]{0:T(1024)}, u32[]{:S(2)}) copy-start(f32[1024]{0:T(1024)} %param.21) | copy-start | bytes 12292
  251.0 10.8 %copy-start.1 = (bf16[16,1,128,1024]{3,2,1,0:T(8,128)(2,1)S(1)}, bf16[16,1,128,1024]{3,2,1,0:T(8,128)(2,1)}, u32[]{:S(2)}) copy-start(bf16[16,1,128,1024]{3,2,1,0:T(8,128)(2,1)} %get-tuple-element.10) | copy-start | bytes 12582916
  268.0 8.5 %copy-start.4 = (bf16[16,2,128,128]{3,2,1,0:T(8,128)(2,1)S(1)}, bf16[16,2,128,128]{3,2,1,0:T(8,128)(2,1)}, u32[]{:S(2)}) copy-start(bf16[16,2,128,128]{3,2,1,0:T(8,128)(2,1)} %param.17) | copy-start | bytes 3145732
  276.5 4.7 %copy-start.11 = (f32[1024]{0:T(1024)S(1)}, f32[1024]{0:T(1024)}, u32[]{:S(2)}) copy-start(f32[1024]{0:T(1024)} %param.24) | copy-start | bytes 12292
  281.3 8.1 %copy-start.8 = (f32[1024]{0:T(1024)S(1)}, f32[1024]{0:T(1024)}, u32[]{:S(2)}) copy-start(f32[1024]{0:T(1024)} %param.25) | copy-start | bytes 12292
where the time goes:
time: 299 us
  waiting for transfers between devices  167 us (56%)
  local copies, waits for them, and re-layouts  40.8 us (14%)
  matrix products  34.5 us (12%)
  starting transfers between devices  28.2 us (9%)
  blocking collectives  14 us (5%)
  other arithmetic  13.3 us (4%)
    all_to_all x1, waiting for transfers between devices, body(): lax.all_to_all(hist_blocks[asked_ids], 'narrow', split_axis=0, concat_axi...  114 us
    ppermute x3, waiting for transfers between devices, shifted(): return lax.ppermute(block, axis, route)  52.7 us
    dot_general x2, matrix products, sage_layer(): summed = jnp.dot(self_rows, w_self, preferred_element_type=jnp.float32)  15.3 us
    ppermute x3, starting transfers between devices, shifted(): return lax.ppermute(block, axis, route)  14.7 us
    all_to_all x1, blocking collectives, body(): lax.all_to_all(jnp.concatenate([near_req, far_req], axis=1), 'narrow', sp...  14 us
    unnamed x27, local copies, waits for them, and re-layouts  13.8 us
    dot_general x2, matrix products, sage_layer(): jnp.dot(mean_rows, w_neighbour, preferred_element_type=jnp.float32)  12.5 us
    all_to_all x1, starting transfers between devices, body(): lax.all_to_all(feat_blocks[asked_ids], 'narrow', split_axis=0, concat_axi...  8.63 us
  transfers between devices with their start and end apart: 5, of which 3 were waited for; matrix products, arithmetic and copies ran while one was open for 14% of the time, Pallas kernels for 0%

commit v1 on v0

v1 whole, which is shorter than its diff:
```python
import functools

import jax
import jax.numpy as jnp
from jax import lax
from jax.experimental import pallas as pl
from jax.experimental.pallas import tpu as pltpu
from jax.sharding import PartitionSpec as P

MESH = pl.DeviceIdType.MESH
REGIONS = 8
SIDE = 4
PEERS = SIDE * SIDE
SLOTS = 2 * PEERS
BLOCK = 128
BLOCKS = 16
FEAT = 128
WIDTH = 1024
ROWS = BLOCKS * BLOCK
GROUPS = ((0, 256), (256, 256), (512, 256), (768, 128), (896, 128))
AHEAD = 3
BF16, F32 = jnp.bfloat16, jnp.float32


def rms_relu(values, gain_row):
    inv_scale = lax.rsqrt(jnp.mean(values * values, axis=-1, keepdims=True) + 1e-06)
    return jnp.maximum(values * inv_scale * gain_row, 0.0).astype(BF16)


def kernel(
    feats_hbm, hist_hbm, src_hbm, count_hbm, edges_hbm,
    w1s_hbm, w1n_hbm, bias_one_ref, gain_one_ref, w2s_hbm, w2n_hbm, bias_two_ref, gain_two_ref,
    fresh_ref, embed_ref,
    feats, hist, edges, w1, w2s, w2n, src, count, want, asked, ids,
    masked, scale, means, total,
    *rest,
):
    groups = 1 + len(GROUPS)
    sends, recvs = rest[:groups], rest[groups : 2 * groups]
    load_sem, req_send, req_recv, send_sem, recv_sem = rest[2 * groups :]
    region, me = lax.axis_index("blk"), lax.axis_index("narrow")
    my_y, my_z = me // SIDE, lax.rem(me, SIDE)
    behind, ahead = lax.rem(region + REGIONS - 1, REGIONS), lax.rem(region + 1, REGIONS)

    loads = [
        pltpu.make_async_copy(a, b, load_sem.at[i])
        for i, (a, b) in enumerate((
            (src_hbm, src), (count_hbm, count), (feats_hbm, feats), (hist_hbm, hist), (edges_hbm, edges),
            (w1s_hbm, w1.at[pl.ds(0, FEAT)]), (w1n_hbm, w1.at[pl.ds(FEAT, FEAT)]), (w2s_hbm, w2s), (w2n_hbm, w2n),
        ))
    ]
    for load in loads:
        load.start()

    barrier = pltpu.get_barrier_semaphore()

    def greet(k, _):
        other = lax.rem(me + k, PEERS)
        pl.semaphore_signal(barrier, inc=1, device_id=(behind, other), device_id_type=MESH)

        @pl.when(k > 0)
        def _():
            pl.semaphore_signal(barrier, inc=1, device_id=(region, other), device_id_type=MESH)

        return 0

    lax.fori_loop(0, PEERS, greet, 0)

    loads[0].wait()

    def slot_of(b, t):
        device = src[t, b] // BLOCKS
        step = lax.rem(device // PEERS - region + REGIONS, REGIONS)
        return jnp.minimum(step, 1) * PEERS + lax.rem(device, PEERS)

    lanes = lax.broadcasted_iota(jnp.int32, (1, 128), 1)
    wanted = jnp.zeros((1, 128), jnp.int32)
    for b in range(BLOCKS):
        for t in range(2):
            wanted = wanted + jnp.where(lanes == slot_of(b, t), lax.rem(src[t, b], BLOCKS), 0)
    want[...] = wanted
    asked[me] = wanted
    pl.semaphore_wait(barrier, SLOTS - 1)

    def ask(k, _):
        other = lax.rem(me + k, PEERS)

        def copy_to(blk, row):
            pltpu.make_async_remote_copy(
                src_ref=want, dst_ref=asked.at[row], send_sem=req_send, recv_sem=req_recv,
                device_id=(blk, other), device_id_type=MESH,
            ).start()

        copy_to(ahead, PEERS + me)

        @pl.when(k > 0)
        def _():
            copy_to(region, me)

        return 0

    lax.fori_loop(0, PEERS, ask, 0)
    all_asked = pltpu.make_async_remote_copy(
        src_ref=asked.at[pl.ds(0, SLOTS - 1)], dst_ref=asked.at[pl.ds(0, SLOTS - 1)],
        send_sem=req_send, recv_sem=req_recv, device_id=(region, lax.rem(me + 1, PEERS)), device_id_type=MESH,
    )
    all_asked.wait_recv()
    to_scalars = pltpu.make_async_copy(asked, ids, load_sem.at[len(loads)])
    to_scalars.start()
    to_scalars.wait()
    loads[2].wait()
    loads[3].wait()

    def picked(g, a):
        local = ids[a, 0, (a // PEERS) * PEERS + me]
        if g == 0:
            return feats[local]
        first, width = GROUPS[g - 1]
        return hist[local, :, first : first + width]

    def send_group(g):
        def step(k, blk, asker_region):
            place = lax.rem(5 * k, PEERS)
            y, z = lax.rem(my_y + place // SIDE, SIDE), lax.rem(my_z + place, SIDE)
            other = y * SIDE + z
            slot = asker_region * PEERS + other
            sends[g][slot] = picked(g, slot)
            pltpu.make_async_remote_copy(
                src_ref=sends[g].at[slot], dst_ref=recvs[g].at[asker_region * PEERS + me],
                send_sem=send_sem.at[g], recv_sem=recv_sem.at[g], device_id=(blk, other), device_id_type=MESH,
            ).start()

        def own(k, _):
            step(k, region, 0)
            return 0

        def previous(k, _):
            step(k, behind, 1)
            return 0

        lax.fori_loop(0, PEERS, previous, 0)
        lax.fori_loop(1, PEERS, own, 0)
        recvs[g][me] = picked(g, me)

    def whole(g):
        return pltpu.make_async_remote_copy(
            src_ref=sends[g].at[pl.ds(0, SLOTS - 1)], dst_ref=recvs[g].at[pl.ds(0, SLOTS - 1)],
            send_sem=send_sem.at[g], recv_sem=recv_sem.at[g],
            device_id=(region, lax.rem(me + 1, PEERS)), device_id_type=MESH,
        )

    for g in range(AHEAD):
        send_group(g)

    for load in loads[4:]:
        load.wait()
    loads[1].wait()

    def mask(b, _):
        for t in range(2):
            live = (t < count[b]).astype(F32)
            masked[b, :, t * BLOCK : (t + 1) * BLOCK] = (edges[b, t].astype(F32) * live).astype(BF16)
        degree = jnp.dot(masked[b], jnp.ones((2 * BLOCK, 128), BF16), preferred_element_type=F32)
        scale[b] = 1.0 / jnp.maximum(degree, 1.0)
        return 0

    lax.fori_loop(0, BLOCKS, mask, 0)

    def mean_of(g, b):
        pair = jnp.concatenate([recvs[g][slot_of(b, 0)], recvs[g][slot_of(b, 1)]], axis=0)
        summed = jnp.dot(masked[b], pair, preferred_element_type=F32)
        width = summed.shape[1]
        return (summed * jnp.concatenate([scale[b]] * (width // 128), axis=1)).astype(BF16)

    def average(g):
        width = recvs[g].shape[2]

        def one(b, _):
            means[pl.ds(pl.multiple_of(b * BLOCK, BLOCK), BLOCK), :width] = mean_of(g, b)
            return 0

        lax.fori_loop(0, BLOCKS, one, 0)

    whole(0).wait_recv()

    def layer_one(b, _):
        rows = pl.ds(pl.multiple_of(b * BLOCK, BLOCK), BLOCK)
        both = jnp.concatenate([feats[b], mean_of(0, b)], axis=1)
        z_one = jnp.dot(both, w1[...], preferred_element_type=F32) + bias_one_ref[...]
        fresh_ref[rows, :] = rms_relu(z_one, gain_one_ref[...])
        return 0

    lax.fori_loop(0, BLOCKS, layer_one, 0)
    TALL = 512

    def own_part(i, _):
        rows = pl.ds(pl.multiple_of(i * TALL, TALL), TALL)
        total[rows, :] = jnp.dot(fresh_ref[rows, :], w2s[...], preferred_element_type=F32) + bias_two_ref[...]
        return 0

    lax.fori_loop(0, ROWS // TALL, own_part, 0)

    for g in range(1, groups - 1):
        if g - 1 + AHEAD < groups:
            send_group(g - 1 + AHEAD)
        whole(g).wait_recv()
        average(g)
        first, width = GROUPS[g - 1]

        def add(i, _):
            rows = pl.ds(pl.multiple_of(i * TALL, TALL), TALL)
            total[rows, :] += jnp.dot(means[rows, :width], w2n[first : first + width, :], preferred_element_type=F32)
            return 0

        lax.fori_loop(0, ROWS // TALL, add, 0)

    g = groups - 1
    whole(g).wait_recv()
    first, width = GROUPS[g - 1]

    def finish(b, _):
        rows = pl.ds(pl.multiple_of(b * BLOCK, BLOCK), BLOCK)
        z_two = total[rows, :] + jnp.dot(mean_of(g, b), w2n[first : first + width, :], preferred_element_type=F32)
        embed_ref[rows, :] = rms_relu(z_two, gain_two_ref[...])
        return 0

    lax.fori_loop(0, BLOCKS, finish, 0)
    for g in range(groups):
        whole(g).wait_send()
    all_asked.wait_send()


def body(
    node_feats, history, tile_src, tile_count, tile_edges,
    w1_self, w1_nbr, bias_one, gain_one, w2_self, w2_nbr, bias_two, gain_two,
):
    widths = [FEAT] + [w for _, w in GROUPS]
    groups = len(widths)
    anywhere, vmem = pl.BlockSpec(memory_space=pl.ANY), pl.BlockSpec(memory_space=pltpu.VMEM)
    return pl.pallas_call(
        kernel,
        out_shape=(pltpu.VMEM((ROWS, WIDTH), BF16), pltpu.VMEM((ROWS, WIDTH), BF16)),
        in_specs=[anywhere] * 7 + [vmem] * 2 + [anywhere] * 2 + [vmem] * 2,
        out_specs=(vmem, vmem),
        scratch_shapes=[
            pltpu.VMEM((BLOCKS, BLOCK, FEAT), BF16),
            pltpu.VMEM((BLOCKS, BLOCK, WIDTH), BF16),
            pltpu.VMEM((BLOCKS, 2, BLOCK, BLOCK), BF16),
            pltpu.VMEM((2 * FEAT, WIDTH), BF16),
            pltpu.VMEM((WIDTH, WIDTH), BF16),
            pltpu.VMEM((WIDTH, WIDTH), BF16),
            pltpu.SMEM((2, BLOCKS), jnp.int32),
            pltpu.SMEM((BLOCKS,), jnp.int32),
            pltpu.VMEM((1, 128), jnp.int32),
            pltpu.VMEM((SLOTS, 1, 128), jnp.int32),
            pltpu.SMEM((SLOTS, 1, 128), jnp.int32),
            pltpu.VMEM((BLOCKS, BLOCK, 2 * BLOCK), BF16),
            pltpu.VMEM((BLOCKS, BLOCK, 128), F32),
            pltpu.VMEM((ROWS, 256), BF16),
            pltpu.VMEM((ROWS, WIDTH), F32),
        ]
        + [pltpu.VMEM((SLOTS, BLOCK, w), BF16) for w in widths] * 2
        + [
            pltpu.SemaphoreType.DMA((10,)),
            pltpu.SemaphoreType.DMA,
            pltpu.SemaphoreType.DMA,
            pltpu.SemaphoreType.DMA((groups,)),
            pltpu.SemaphoreType.DMA((groups,)),
        ],
        compiler_params=pltpu.CompilerParams(collective_id=0, has_side_effects=True, vmem_limit_bytes=48 << 20),
        name="sage",
    )(
        node_feats.reshape(BLOCKS, BLOCK, FEAT), history.reshape(BLOCKS, BLOCK, WIDTH), tile_src.T, tile_count,
        tile_edges, w1_self, w1_nbr, bias_one.reshape(1, WIDTH), gain_one.reshape(1, WIDTH), w2_self, w2_nbr,
        bias_two.reshape(1, WIDTH), gain_two.reshape(1, WIDTH),
    )


def solution(mesh):
    nodes = P(("blk", "narrow"), None)
    return jax.shard_map(
        body,
        mesh=mesh,
        in_specs=(nodes, nodes, nodes, P(("blk", "narrow")), P(("blk", "narrow"), None, None, None)) + (P(),) * 8,
        out_specs=(nodes, nodes),
        check_vma=False,
    )
```

time: 299 us -> 134 us (0.45)
  waiting for transfers between devices: 167 us -> 0 us
  Pallas kernels: 0 us -> 127 us
  local copies, waits for them, and re-layouts: 40.8 us -> 4.03 us
  matrix products: 34.5 us -> 0 us
  starting transfers between devices: 28.2 us -> 0 us
  blocking collectives: 14 us -> 0 us
  other arithmetic: 13.3 us -> 0 us
    pallas_call x0 -> x1, Pallas kernels: none -> 127 us  [body(): pl.pallas_call(kernel, out_shape=(pltpu.VMEM((ROWS, WIDTH), BF16), pltpu....]
    all_to_all x2 -> x0, waiting for transfers between devices: 114 us -> none  [the longest x1 114 us: body(): lax.all_to_all(hist_blocks[asked_ids], 'narrow', split_axis=0, concat_axi...]
    ppermute x3 -> x0, waiting for transfers between devices: 52.7 us -> none  [shifted(): return lax.ppermute(block, axis, route)]
    dot_general x6 -> x0, matrix products: 34.5 us -> none  [the longest x2 15.3 us: sage_layer(): summed = jnp.dot(self_rows, w_self, preferred_element_type=jnp.float32)]
    gather x4 -> x0, local copies, waits for them, and re-layouts: 18.8 us -> none  [the longest x1 8.48 us: body(): got_hist.reshape(tile_total, block_rows, history.shape[1])[slot_index]]
    ppermute x3 -> x0, starting transfers between devices: 14.7 us -> none  [shifted(): return lax.ppermute(block, axis, route)]
    all_to_all x1 -> x0, blocking collectives: 14 us -> none  [body(): lax.all_to_all(jnp.concatenate([near_req, far_req], axis=1), 'narrow', sp...]
    all_to_all x2 -> x0, starting transfers between devices: 13.5 us -> none  [the longest x1 8.63 us: body(): lax.all_to_all(feat_blocks[asked_ids], 'narrow', split_axis=0, concat_axi...]
  transfers between devices with their start and end apart: 5 -> 0, of which waited for: 3 -> 0; matrix products, arithmetic and copies ran while one was open for 14% -> 0% of each run, Pallas kernels for 0% -> 0%
where the time goes in v1:
time: 134 us; the launch traced here: 132 us
  Pallas kernels  127 us (95%)
  local copies, waits for them, and re-layouts  4.03 us (3%)
    pallas_call x1, Pallas kernels, body(): pl.pallas_call(kernel, out_shape=(pltpu.VMEM((ROWS, WIDTH), BF16), pltpu....  127 us
    unnamed x2, local copies, waits for them, and re-layouts  4.03 us

profile of v1, /device:TPU:1, one launch (start us, length us, event | category | flops | bytes accessed | tf_op | source)
XLA Modules:
  0.0 131.9 jit_solution(2706335678710441574)
XLA Ops:
  0.6 127.3 %sage.1 = (bf16[2048,1024]{1,0:T(8,128)(2,1)S(1)}, bf16[2048,1024]{1,0:T(8,128)(2,1)S(1)}) custom-call(bf16[16,128,128]{2,1,0:T(8,128)(2,1)} %bitcast.8, bf16[16,128,1024]{2,1,0:T(8,128)(2,1)} %bitcast.7, s32[2,16]{1,0:T(2,128)} %bitcast.13, s32[16]{0:T(128)} %count_hbm.1, bf16[16,2,128,128]{3,2,1,0:T(8,128)(2,1)} %edges_hbm.1, bf16[128,1024]{1,0:T(8,128)(2,1)} %w1s_hbm.1, ...), custom_call_target="tpu_custom_call" | custom-call | tf_op jit(solution)/shard_map/sage/pallas_call | solution.py:240
  127.9 2.0 %copy.17 = bf16[2048,1024]{1,0:T(8,128)(2,1)} copy(bf16[2048,1024]{1,0:T(8,128)(2,1)S(1)} %get-tuple-element.2) | data formatting | bytes 8388608
  129.9 2.0 %copy.18 = bf16[2048,1024]{1,0:T(8,128)(2,1)} copy(bf16[2048,1024]{1,0:T(8,128)(2,1)S(1)} %get-tuple-element.3) | data formatting | bytes 8388608

commit v2 on v1

--- a/solution.py
+++ b/solution.py
@@ -18,7 +18,8 @@
 WIDTH = 1024
 ROWS = BLOCKS * BLOCK
 GROUPS = ((0, 256), (256, 256), (512, 256), (768, 128), (896, 128))
-AHEAD = 3
+TALL = 512
+AHEAD = 6
 BF16, F32 = jnp.bfloat16, jnp.float32
 
 
@@ -29,10 +30,10 @@
 
 def kernel(
     feats_hbm, hist_hbm, src_hbm, count_hbm, edges_hbm,
-    w1s_hbm, w1n_hbm, bias_one_ref, gain_one_ref, w2s_hbm, w2n_hbm, bias_two_ref, gain_two_ref,
-    fresh_ref, embed_ref,
+    w1s_hbm, w1n_hbm, bias_one_hbm, gain_one_hbm, w2s_hbm, w2n_hbm, bias_two_hbm,
+    fresh_ref, total, last_means, last_w2n,
     feats, hist, edges, w1, w2s, w2n, src, count, want, asked, ids,
-    masked, scale, means, total,
+    bias_one_ref, gain_one_ref, bias_two_ref, masked, scale, means,
     *rest,
 ):
     groups = 1 + len(GROUPS)
@@ -47,6 +48,7 @@
         for i, (a, b) in enumerate((
             (src_hbm, src), (count_hbm, count), (feats_hbm, feats), (hist_hbm, hist), (edges_hbm, edges),
             (w1s_hbm, w1.at[pl.ds(0, FEAT)]), (w1n_hbm, w1.at[pl.ds(FEAT, FEAT)]), (w2s_hbm, w2s), (w2n_hbm, w2n),
+            (bias_one_hbm, bias_one_ref), (gain_one_hbm, gain_one_ref), (bias_two_hbm, bias_two_ref),
         ))
     ]
     for load in loads:
@@ -172,14 +174,14 @@
         width = summed.shape[1]
         return (summed * jnp.concatenate([scale[b]] * (width // 128), axis=1)).astype(BF16)
 
-    def average(g):
+    def average(g, means):
         width = recvs[g].shape[2]
 
         def one(b, _):
             means[pl.ds(pl.multiple_of(b * BLOCK, BLOCK), BLOCK), :width] = mean_of(g, b)
             return 0
 
-        lax.fori_loop(0, BLOCKS, one, 0)
+        lax.fori_loop(0, BLOCKS, one, 0, unroll=4)
 
     whole(0).wait_recv()
 
@@ -191,8 +193,6 @@
         return 0
 
     lax.fori_loop(0, BLOCKS, layer_one, 0)
-    TALL = 512
-
     def own_part(i, _):
         rows = pl.ds(pl.multiple_of(i * TALL, TALL), TALL)
         total[rows, :] = jnp.dot(fresh_ref[rows, :], w2s[...], preferred_element_type=F32) + bias_two_ref[...]
@@ -204,7 +204,7 @@
         if g - 1 + AHEAD < groups:
             send_group(g - 1 + AHEAD)
         whole(g).wait_recv()
-        average(g)
+        average(g, means)
         first, width = GROUPS[g - 1]
 
         def add(i, _):
@@ -215,19 +215,29 @@
         lax.fori_loop(0, ROWS // TALL, add, 0)
 
     g = groups - 1
+    first, width = GROUPS[g - 1]
+    last_w2n[...] = w2n[first : first + width, :]
     whole(g).wait_recv()
-    first, width = GROUPS[g - 1]
-
-    def finish(b, _):
-        rows = pl.ds(pl.multiple_of(b * BLOCK, BLOCK), BLOCK)
-        z_two = total[rows, :] + jnp.dot(mean_of(g, b), w2n[first : first + width, :], preferred_element_type=F32)
-        embed_ref[rows, :] = rms_relu(z_two, gain_two_ref[...])
-        return 0
-
-    lax.fori_loop(0, BLOCKS, finish, 0)
+    average(g, last_means)
     for g in range(groups):
         whole(g).wait_send()
     all_asked.wait_send()
+
+
+def finish(total, means, w2n, fresh, gain_ref, fresh_hbm, embed_hbm, staged, sems):
+    pass_on = pltpu.make_async_copy(fresh, fresh_hbm, sems.at[0])
+    pass_on.start()
+
+    def step(i, _):
+        rows = pl.ds(pl.multiple_of(i * TALL, TALL), TALL)
+        z_two = total[rows, :] + jnp.dot(means[rows, :], w2n[...], preferred_element_type=F32)
+        staged[rows, :] = rms_relu(z_two, gain_ref[...])
+        pltpu.make_async_copy(staged.at[rows], embed_hbm.at[rows], sems.at[1]).start()
+        return 0
+
+    lax.fori_loop(0, ROWS // TALL, step, 0)
+    pltpu.make_async_copy(staged, embed_hbm, sems.at[1]).wait()
+    pass_on.wait()
 
 
 def body(
@@ -236,12 +246,23 @@
 ):
     widths = [FEAT] + [w for _, w in GROUPS]
     groups = len(widths)
-    anywhere, vmem = pl.BlockSpec(memory_space=pl.ANY), pl.BlockSpec(memory_space=pltpu.VMEM)
-    return pl.pallas_call(
+    hbm, vmem = pl.BlockSpec(memory_space=pltpu.HBM), pl.BlockSpec(memory_space=pltpu.VMEM)
+    last = widths[-1]
+    operands = (
+        node_feats.reshape(BLOCKS, BLOCK, FEAT), history.reshape(BLOCKS, BLOCK, WIDTH), tile_src.T, tile_count,
+        tile_edges, w1_self, w1_nbr, bias_one.reshape(1, WIDTH), gain_one.reshape(1, WIDTH), w2_self, w2_nbr,
+        bias_two.reshape(1, WIDTH),
+    )
+    fresh, total, means, w2n_rows = pl.pallas_call(
         kernel,
-        out_shape=(pltpu.VMEM((ROWS, WIDTH), BF16), pltpu.VMEM((ROWS, WIDTH), BF16)),
-        in_specs=[anywhere] * 7 + [vmem] * 2 + [anywhere] * 2 + [vmem] * 2,
-        out_specs=(vmem, vmem),
+        out_shape=(
+            pltpu.VMEM((ROWS, WIDTH), BF16),
+            pltpu.VMEM((ROWS, WIDTH), F32),
+            pltpu.VMEM((ROWS, last), BF16),
+            pltpu.VMEM((last, WIDTH), BF16),
+        ),
+        in_specs=[hbm] * 12,
+        out_specs=(vmem,) * 4,
         scratch_shapes=[
             pltpu.VMEM((BLOCKS, BLOCK, FEAT), BF16),
             pltpu.VMEM((BLOCKS, BLOCK, WIDTH), BF16),
@@ -254,26 +275,36 @@
             pltpu.VMEM((1, 128), jnp.int32),
             pltpu.VMEM((SLOTS, 1, 128), jnp.int32),
             pltpu.SMEM((SLOTS, 1, 128), jnp.int32),
+            pltpu.VMEM((1, WIDTH), F32),
+            pltpu.VMEM((1, WIDTH), F32),
+            pltpu.VMEM((1, WIDTH), F32),
             pltpu.VMEM((BLOCKS, BLOCK, 2 * BLOCK), BF16),
             pltpu.VMEM((BLOCKS, BLOCK, 128), F32),
             pltpu.VMEM((ROWS, 256), BF16),
-            pltpu.VMEM((ROWS, WIDTH), F32),
         ]
         + [pltpu.VMEM((SLOTS, BLOCK, w), BF16) for w in widths] * 2
         + [
-            pltpu.SemaphoreType.DMA((10,)),
+            pltpu.SemaphoreType.DMA((13,)),
             pltpu.SemaphoreType.DMA,
             pltpu.SemaphoreType.DMA,
             pltpu.SemaphoreType.DMA((groups,)),
             pltpu.SemaphoreType.DMA((groups,)),
         ],
-        compiler_params=pltpu.CompilerParams(collective_id=0, has_side_effects=True, vmem_limit_bytes=48 << 20),
+        compiler_params=pltpu.CompilerParams(collective_id=0, has_side_effects=True, vmem_limit_bytes=40 << 20),
         name="sage",
     )(
-        node_feats.reshape(BLOCKS, BLOCK, FEAT), history.reshape(BLOCKS, BLOCK, WIDTH), tile_src.T, tile_count,
-        tile_edges, w1_self, w1_nbr, bias_one.reshape(1, WIDTH), gain_one.reshape(1, WIDTH), w2_self, w2_nbr,
-        bias_two.reshape(1, WIDTH), gain_two.reshape(1, WIDTH),
+        *(pltpu.with_memory_space_constraint(a, pltpu.HBM) for a in operands)
     )
+    rows = jax.ShapeDtypeStruct((ROWS, WIDTH), BF16)
+    return pl.pallas_call(
+        finish,
+        out_shape=(rows, rows),
+        in_specs=[vmem] * 5,
+        out_specs=(hbm,) * 2,
+        scratch_shapes=[pltpu.VMEM((ROWS, WIDTH), BF16), pltpu.SemaphoreType.DMA((2,))],
+        compiler_params=pltpu.CompilerParams(vmem_limit_bytes=12 << 20),
+        name="finish",
+    )(total, means, w2n_rows, fresh, gain_two.reshape(1, WIDTH))
 
 
 def solution(mesh):

time: 134 us -> 124 us (0.925); the launches traced: 132 us -> 124 us
  local copies, waits for them, and re-layouts: 4.03 us -> 0.01 us
  Pallas kernels: 127 us -> 123 us
    pallas_call x1, Pallas kernels: 127 us -> 120 us  [body(): pl.pallas_call(kernel, out_shape=(pltpu.VMEM((ROWS, WIDTH), BF16), pltpu....]
    unnamed x2, local copies, waits for them, and re-layouts: 4.03 us -> 0.01 us
    pallas_call x0 -> x1, Pallas kernels: none -> 3.88 us  [body(): pl.pallas_call(finish, out_shape=(rows, rows), in_specs=[vmem] * 5, out_s...]
where the time goes in v2:
time: 124 us
  Pallas kernels  123 us (99%)
    pallas_call x1, Pallas kernels, body(): pl.pallas_call(kernel, out_shape=(pltpu.VMEM((ROWS, WIDTH), BF16), pltpu....  120 us
    pallas_call x1, Pallas kernels, body(): pl.pallas_call(finish, out_shape=(rows, rows), in_specs=[vmem] * 5, out_s...  3.88 us

profile of v2, /device:TPU:1, one launch (start us, length us, event | category | flops | bytes accessed | tf_op | source)
XLA Modules:
  0.0 124.1 jit_solution(13965833181879131618)
XLA Ops:
  0.6 0.0 copy-start
  0.6 119.6 %sage.1 = (bf16[2048,1024]{1,0:T(8,128)(2,1)S(1)}, f32[2048,1024]{1,0:T(8,128)S(1)}, bf16[2048,128]{1,0:T(8,128)(2,1)S(1)}, bf16[128,1024]{1,0:T(8,128)(2,1)S(1)}) custom-call(bf16[16,128,128]{2,1,0:T(8,128)(2,1)} %bitcast.9, bf16[16,128,1024]{2,1,0:T(8,128)(2,1)} %bitcast.8, s32[2,16]{1,0:T(2,128)} %bitcast.13, s32[16]{0:T(128)} %count_hbm.1, ...), custom_call_target="tpu_custom_call" | custom-call | tf_op jit(solution)/shard_map/sage/pallas_call | solution.py:256
  120.2 0.0 copy-done
  120.2 3.9 %finish.1 = (bf16[2048,1024]{1,0:T(8,128)(2,1)}, bf16[2048,1024]{1,0:T(8,128)(2,1)}) custom-call(f32[2048,1024]{1,0:T(8,128)S(1)} %get-tuple-element.6.total, bf16[2048,128]{1,0:T(8,128)(2,1)S(1)} %get-tuple-element.7.means, bf16[128,1024]{1,0:T(8,128)(2,1)S(1)} %get-tuple-element.8.w2n, bf16[2048,1024]{1,0:T(8,128)(2,1)S(1)} %get-tuple-element.9.fresh, ...), custom_call_target="tpu_custom_call" | custom-call | tf_op jit(solution)/shard_map/finish/pallas_call | solution.py:299
Async XLA Ops:
  0.6 119.6 %copy-start = (f32[1024]{0:T(1024)S(1)}, f32[1024]{0:T(1024)}, u32[]{:S(2)}) copy-start(f32[1024]{0:T(1024)} %param.25) | copy-start | bytes 12292

commit v3 on v2

--- a/solution.py
+++ b/solution.py
@@ -140,8 +140,8 @@
             step(k, behind, 1)
             return 0
 
+        lax.fori_loop(1, PEERS, own, 0)
         lax.fori_loop(0, PEERS, previous, 0)
-        lax.fori_loop(1, PEERS, own, 0)
         recvs[g][me] = picked(g, me)
 
     def whole(g):
@@ -235,7 +235,7 @@
         pltpu.make_async_copy(staged.at[rows], embed_hbm.at[rows], sems.at[1]).start()
         return 0
 
-    lax.fori_loop(0, ROWS // TALL, step, 0)
+    lax.fori_loop(0, ROWS // TALL, step, 0, unroll=True)
     pltpu.make_async_copy(staged, embed_hbm, sems.at[1]).wait()
     pass_on.wait()
 

time: 124 us -> 122 us (0.984); the launches traced: 124 us -> 120 us
  Pallas kernels: 123 us -> 120 us
    pallas_call x1, Pallas kernels: 120 us -> 116 us  [body(): pl.pallas_call(kernel, out_shape=(pltpu.VMEM((ROWS, WIDTH), BF16), pltpu....]
where the time goes in v3:
time: 122 us; the launch traced here: 120 us
  Pallas kernels  120 us (98%)
    pallas_call x1, Pallas kernels, body(): pl.pallas_call(kernel, out_shape=(pltpu.VMEM((ROWS, WIDTH), BF16), pltpu....  116 us
    pallas_call x1, Pallas kernels, body(): pl.pallas_call(finish, out_shape=(rows, rows), in_specs=[vmem] * 5, out_s...  3.39 us

profile of v3, /device:TPU:1, one launch (start us, length us, event | category | flops | bytes accessed | tf_op | source)
XLA Modules:
  0.0 120.2 jit_solution(3602908627705884497)
XLA Ops:
  0.6 0.0 copy-start
  0.6 116.1 %sage.1 = (bf16[2048,1024]{1,0:T(8,128)(2,1)S(1)}, f32[2048,1024]{1,0:T(8,128)S(1)}, bf16[2048,128]{1,0:T(8,128)(2,1)S(1)}, bf16[128,1024]{1,0:T(8,128)(2,1)S(1)}) custom-call(bf16[16,128,128]{2,1,0:T(8,128)(2,1)} %bitcast.9, bf16[16,128,1024]{2,1,0:T(8,128)(2,1)} %bitcast.8, s32[2,16]{1,0:T(2,128)} %bitcast.13, s32[16]{0:T(128)} %count_hbm.1, ...), custom_call_target="tpu_custom_call" | custom-call | tf_op jit(solution)/shard_map/sage/pallas_call | solution.py:256
  116.8 0.0 copy-done
  116.8 3.4 %finish.1 = (bf16[2048,1024]{1,0:T(8,128)(2,1)}, bf16[2048,1024]{1,0:T(8,128)(2,1)}) custom-call(f32[2048,1024]{1,0:T(8,128)S(1)} %get-tuple-element.6.total, bf16[2048,128]{1,0:T(8,128)(2,1)S(1)} %get-tuple-element.7.means, bf16[128,1024]{1,0:T(8,128)(2,1)S(1)} %get-tuple-element.8.w2n, bf16[2048,1024]{1,0:T(8,128)(2,1)S(1)} %get-tuple-element.9.fresh, ...), custom_call_target="tpu_custom_call" | custom-call | tf_op jit(solution)/shard_map/finish/pallas_call | solution.py:299
Async XLA Ops:
  0.6 116.2 %copy-start = (f32[1024]{0:T(1024)S(1)}, f32[1024]{0:T(1024)}, u32[]{:S(2)}) copy-start(f32[1024]{0:T(1024)} %param.25) | copy-start | bytes 12292

commit v4 on v3

--- a/solution.py
+++ b/solution.py
@@ -85,7 +85,8 @@
     pl.semaphore_wait(barrier, SLOTS - 1)
 
     def ask(k, _):
-        other = lax.rem(me + k, PEERS)
+        place = lax.rem(14 + 15 * k, PEERS)
+        other = lax.rem(my_y + place // SIDE, SIDE) * SIDE + lax.rem(my_z + place, SIDE)
 
         def copy_to(blk, row):
             pltpu.make_async_remote_copy(
@@ -95,7 +96,7 @@
 
         copy_to(ahead, PEERS + me)
 
-        @pl.when(k > 0)
+        @pl.when(place > 0)
         def _():
             copy_to(region, me)
 
@@ -174,14 +175,14 @@
         width = summed.shape[1]
         return (summed * jnp.concatenate([scale[b]] * (width // 128), axis=1)).astype(BF16)
 
-    def average(g, means):
+    def average(g, means, together):
         width = recvs[g].shape[2]
 
         def one(b, _):
             means[pl.ds(pl.multiple_of(b * BLOCK, BLOCK), BLOCK), :width] = mean_of(g, b)
             return 0
 
-        lax.fori_loop(0, BLOCKS, one, 0, unroll=4)
+        lax.fori_loop(0, BLOCKS, one, 0, unroll=together)
 
     whole(0).wait_recv()
 
@@ -204,7 +205,7 @@
         if g - 1 + AHEAD < groups:
             send_group(g - 1 + AHEAD)
         whole(g).wait_recv()
-        average(g, means)
+        average(g, means, 4)
         first, width = GROUPS[g - 1]
 
         def add(i, _):
@@ -218,7 +219,7 @@
     first, width = GROUPS[g - 1]
     last_w2n[...] = w2n[first : first + width, :]
     whole(g).wait_recv()
-    average(g, last_means)
+    average(g, last_means, BLOCKS)
     for g in range(groups):
         whole(g).wait_send()
     all_asked.wait_send()

time: 122 us -> 122 us (level)
  no operation moved by 1% of the time
where the time goes in v4:
time: 122 us; the launch traced here: 120 us
  Pallas kernels  119 us (98%)
    pallas_call x1, Pallas kernels, body(): pl.pallas_call(kernel, out_shape=(pltpu.VMEM((ROWS, WIDTH), BF16), pltpu....  116 us
    pallas_call x1, Pallas kernels, body(): pl.pallas_call(finish, out_shape=(rows, rows), in_specs=[vmem] * 5, out_s...  3.38 us

profile of v4, /device:TPU:1, one launch (start us, length us, event | category | flops | bytes accessed | tf_op | source)
XLA Modules:
  0.0 119.7 jit_solution(16700779692801271020)
XLA Ops:
  0.6 0.0 copy-start
  0.6 115.7 %sage.1 = (bf16[2048,1024]{1,0:T(8,128)(2,1)S(1)}, f32[2048,1024]{1,0:T(8,128)S(1)}, bf16[2048,128]{1,0:T(8,128)(2,1)S(1)}, bf16[128,1024]{1,0:T(8,128)(2,1)S(1)}) custom-call(bf16[16,128,128]{2,1,0:T(8,128)(2,1)} %bitcast.9, bf16[16,128,1024]{2,1,0:T(8,128)(2,1)} %bitcast.8, s32[2,16]{1,0:T(2,128)} %bitcast.13, s32[16]{0:T(128)} %count_hbm.1, ...), custom_call_target="tpu_custom_call" | custom-call | tf_op jit(solution)/shard_map/sage/pallas_call | solution.py:257
  116.3 0.0 copy-done
  116.3 3.4 %finish.1 = (bf16[2048,1024]{1,0:T(8,128)(2,1)}, bf16[2048,1024]{1,0:T(8,128)(2,1)}) custom-call(f32[2048,1024]{1,0:T(8,128)S(1)} %get-tuple-element.6.total, bf16[2048,128]{1,0:T(8,128)(2,1)S(1)} %get-tuple-element.7.means, bf16[128,1024]{1,0:T(8,128)(2,1)S(1)} %get-tuple-element.8.w2n, bf16[2048,1024]{1,0:T(8,128)(2,1)S(1)} %get-tuple-element.9.fresh, ...), custom_call_target="tpu_custom_call" | custom-call | tf_op jit(solution)/shard_map/finish/pallas_call | solution.py:300
Async XLA Ops:
  0.6 115.7 %copy-start = (f32[1024]{0:T(1024)S(1)}, f32[1024]{0:T(1024)}, u32[]{:S(2)}) copy-start(f32[1024]{0:T(1024)} %param.25) | copy-start | bytes 12292
